TPU v7x, 32 devices: a whole 2x2x4 slice. The times are simulated.
32 devices in a mesh: tx: 8 (over y, x, core), ty: 4 (over z).
Axes of the slice: x: 2, y: 2, z: 4, core: 2. Of those that a mesh axis runs over, the one named last changes fastest.
Arguments:
- points: float32 [3, 65536], P(None, ('tx', 'ty')), may hold values from 0 to 1
- tree_order: int32 [32, 2048], P(('tx', 'ty')), may hold values from 0 to 2047, each once within a row
- samples: float32 [65536, 128], P(('tx', 'ty')), may hold values from -6 to 6
- near_leaves: int32 [256, 5], P(('tx', 'ty')), may hold values from 0 to 11, as said below
- near_counts: int32 [256], P(('tx', 'ty')), may hold values from 0 to 5, as said below
Outputs:
- leaf_bases: float32 [65536, 128], P(('tx', 'ty'))
- local_bases: float32 [224, 256, 128], P(('tx', 'ty'))
- upper_bases: float32 [160, 256, 128], P(('tx', 'ty'))
- root_factor: float32 [128, 128], replicated
Inputs may be any that keep to these rules, and one draw needn't show every extreme that they name: `near_leaves`: for k < near_counts[i], the entry w at [i, k] names the existing leaf (i // 8) * 8 - 2 + w, which is not i; the leaves named in one row are distinct; entries at k >= near_counts[i] are 0. `near_counts`: leaf 0 lists exactly 5 near-field leaves in every draw. `tree_order`: each row is a permutation of the positions of one device's block.
All inputs are finite; a program needn't handle non-finite values.
Results may differ from a plain program's by a relative error of at most 0.0003.
Values sent between devices are 32-bit elements; how exact they have to be, the bound alone decides.
A program may use at most 64 MiB of HBM per device.

v0:
```python
import functools

import jax
import jax.numpy as jnp
from jax import lax
from jax.experimental import pallas as pl
from jax.experimental.pallas import tpu as pltpu
from jax.sharding import PartitionSpec as P

HALO = 2
MAXNB = 5
PANEL = 32


SPREAD = 50.0


def from_partner(value, axis, stride):
    mask = 2**stride
    pairs = [(source, source ^ mask) for source in range(lax.axis_size(axis))]
    return lax.ppermute(value, axis, pairs)


def dot(a, b, contract_a=1, contract_b=0):
    return lax.dot_general(
        a,
        b,
        (((contract_a,), (contract_b,)), ((), ())),
        precision=lax.Precision.HIGHEST,
        preferred_element_type=jnp.float32,
    )


def linear_position():
    return lax.axis_index("tx") * lax.axis_size("ty") + lax.axis_index("ty")


def device_at(position):
    across = lax.axis_size("ty")
    return (position // across, position % across)


def sample_kernel(
    near_ref, count_ref, points_ref, order_ref, samples_ref, sampled_ref, gram_ref,
    ordered, before_points, after_points, before_samples, after_samples,
    rows, columns, pieces, tile, send_sems, recv_sems,
):
    me = linear_position()
    devices = lax.axis_size("tx") * lax.axis_size("ty")
    has_before, has_after = me > 0, me < devices - 1
    leaves, leaf_size, rank = sampled_ref.shape
    lines = leaf_size // 128
    edge = HALO * leaf_size

    barrier = pltpu.get_barrier_semaphore()

    @pl.when(has_before)
    def _():
        pl.semaphore_signal(
            barrier, inc=1, device_id=device_at(me - 1), device_id_type=pl.DeviceIdType.MESH
        )

    @pl.when(has_after)
    def _():
        pl.semaphore_signal(
            barrier, inc=1, device_id=device_at(me + 1), device_id_type=pl.DeviceIdType.MESH
        )

    order = order_ref[...]
    place, line = order % 128, order // 128
    for coord in range(3):
        picked = jnp.zeros(order.shape, jnp.float32)
        for a in range(order.shape[0]):
            source = jnp.broadcast_to(points_ref[coord, a : a + 1, :], order.shape)
            gathered = jnp.take_along_axis(source, place, axis=1, mode="promise_in_bounds")
            picked = jnp.where(line == a, gathered, picked)
        ordered[coord] = picked

    pl.semaphore_wait(barrier, has_before.astype(jnp.int32) + has_after.astype(jnp.int32))

    def copy(index, source, target, position):
        return pltpu.make_async_remote_copy(
            src_ref=source,
            dst_ref=target,
            send_sem=send_sems.at[index],
            recv_sem=recv_sems.at[index],
            device_id=device_at(position),
            device_id_type=pl.DeviceIdType.MESH,
        )

    own_rows = samples_ref.shape[0]
    to_after = [
        copy(0, samples_ref.at[pl.ds(own_rows - edge, edge)], before_samples, me + 1),
        copy(1, ordered, before_points, me + 1),
    ]
    to_before = [
        copy(2, samples_ref.at[pl.ds(0, edge)], after_samples, me - 1),
        copy(3, ordered, after_points, me - 1),
    ]

    @pl.when(has_after)
    def _():
        for c in to_after:
            c.start()

    @pl.when(has_before)
    def _():
        for c in to_before:
            c.start()

    def place_leaf(window_leaf, points, leaf, samples):
        for coord in range(3):
            rows[window_leaf, coord : coord + 1, :] = jnp.concatenate(
                [points[coord, leaf * lines + n : leaf * lines + n + 1, :] for n in range(lines)],
                axis=1,
            )
        high = samples.astype(jnp.bfloat16)
        low = (samples - high.astype(jnp.float32)).astype(jnp.bfloat16)
        pieces[window_leaf] = jnp.concatenate([high, low], axis=1)

    for leaf in range(leaves):
        place_leaf(
            HALO + leaf, ordered, leaf, samples_ref[leaf * leaf_size : (leaf + 1) * leaf_size, :]
        )
        for coord in range(3):
            for n in range(lines):
                wide = jnp.broadcast_to(
                    ordered[coord, leaf * lines + n : leaf * lines + n + 1, :], (128, 128)
                )
                columns[coord, leaf, n * 128 : (n + 1) * 128, :] = wide.T

    def tile_product(leaf, window_leaf, weight):
        others = rows[window_leaf]
        chunk = 64
        for start in range(0, leaf_size, chunk):
            distance = 0.0
            for coord in range(3):
                own = columns[coord, leaf, start : start + chunk, :]
                own = jnp.concatenate([own] * lines, axis=1)
                gap = own - others[coord : coord + 1, :]
                distance = distance + gap * gap
            value = jnp.exp(-SPREAD * distance)
            if weight is not None:
                value = value * weight
            high = value.astype(jnp.bfloat16)
            low = (value - high.astype(jnp.float32)).astype(jnp.bfloat16)
            tile[start : start + chunk, :] = high
            tile[leaf_size + start : leaf_size + start + chunk, :] = low
        product = lax.dot_general(
            tile[...],
            pieces[window_leaf],
            (((1,), (0,)), ((), ())),
            preferred_element_type=jnp.float32,
        )
        product = product[:leaf_size] + product[leaf_size:]
        return product[:, :rank] + product[:, rank:]

    @pl.loop(0, leaves)
    def _(leaf):
        sampled_ref[leaf] = tile_product(leaf, HALO + leaf, None)

    @pl.when(has_before)
    def _():
        copy(0, samples_ref.at[pl.ds(0, edge)], before_samples, me - 1).wait_recv()
        copy(1, ordered, before_points, me - 1).wait_recv()

    @pl.when(has_after)
    def _():
        copy(2, samples_ref.at[pl.ds(0, edge)], after_samples, me + 1).wait_recv()
        copy(3, ordered, after_points, me + 1).wait_recv()

    @pl.when(jnp.logical_not(has_before))
    def _():
        before_samples[...] = jnp.zeros_like(before_samples)
        before_points[...] = jnp.zeros_like(before_points)

    @pl.when(jnp.logical_not(has_after))
    def _():
        after_samples[...] = jnp.zeros_like(after_samples)
        after_points[...] = jnp.zeros_like(after_points)

    for h in range(HALO):
        part = slice(h * leaf_size, (h + 1) * leaf_size)
        place_leaf(h, before_points, leaves - HALO + h, before_samples[part, :])
        place_leaf(HALO + leaves + h, after_points, h, after_samples[part, :])

    @pl.loop(0, leaves)
    def _(leaf):
        total = sampled_ref[leaf]
        for k in range(MAXNB):
            weight = (count_ref[leaf] > k).astype(jnp.float32)
            total = total + tile_product(leaf, near_ref[leaf, k], weight)
        sampled_ref[leaf] = total
        gram_ref[leaf] = dot(total, total, 0, 0)

    @pl.when(has_after)
    def _():
        for c in to_after:
            c.wait_send()

    @pl.when(has_before)
    def _():
        for c in to_before:
            c.wait_send()


def sample_leaves(points, tree_order, samples, near_leaves, near_counts):
    leaves = near_counts.shape[0]
    rank = samples.shape[1]
    leaf_size = samples.shape[0] // leaves
    lines = points.shape[1] // 128
    window = leaves + 2 * HALO
    edge = HALO * leaf_size
    vmem = pl.BlockSpec(memory_space=pltpu.VMEM)
    smem = pl.BlockSpec(memory_space=pltpu.SMEM)
    block = (3, lines, 128)
    return pl.pallas_call(
        sample_kernel,
        out_shape=(
            jax.ShapeDtypeStruct((leaves, leaf_size, rank), jnp.float32),
            jax.ShapeDtypeStruct((leaves, rank, rank), jnp.float32),
        ),
        in_specs=[smem, smem, vmem, vmem, vmem],
        out_specs=(vmem, vmem),
        scratch_shapes=[
            pltpu.VMEM(block, jnp.float32),
            pltpu.VMEM(block, jnp.float32),
            pltpu.VMEM(block, jnp.float32),
            pltpu.VMEM((edge, rank), jnp.float32),
            pltpu.VMEM((edge, rank), jnp.float32),
            pltpu.VMEM((window, 8, leaf_size), jnp.float32),
            pltpu.VMEM((3, leaves, leaf_size, 128), jnp.float32),
            pltpu.VMEM((window, leaf_size, 2 * rank), jnp.bfloat16),
            pltpu.VMEM((2 * leaf_size, leaf_size), jnp.bfloat16),
            pltpu.SemaphoreType.DMA((4,)),
            pltpu.SemaphoreType.DMA((4,)),
        ],
        compiler_params=pltpu.CompilerParams(
            vmem_limit_bytes=40 * 2**20, collective_id=0, has_side_effects=True
        ),
        name="sample_leaves",
    )(
        near_leaves,
        near_counts,
        points.reshape(block),
        tree_order.reshape(lines, 128),
        samples,
    )


def eliminate(work, first, count):
    size = work.shape[-1]
    chunks = PANEL // 8
    lane = lax.broadcasted_iota(jnp.int32, (1, 1, size), 2)
    sub = lax.broadcasted_iota(jnp.int32, (1, 8, size), 1)
    group = pl.ds(first, count)
    for top in range(0, size, PANEL):
        parts = [work[group, top + 8 * t : top + 8 * t + 8, :] for t in range(chunks)]
        for k in range(PANEL):
            own, s = k // 8, k % 8
            here = lane == top + k
            columns = {
                t: jnp.broadcast_to(parts[t][:, :, top + k : top + k + 1], parts[t].shape)
                for t in range(own, chunks)
            }
            d = columns[own][:, s : s + 1, :]
            r = lax.rsqrt(d)
            r = r * (1.5 - 0.5 * d * r * r)
            row = jnp.where(here, r, parts[own][:, s : s + 1, :] * r)
            for t in range(own, chunks):
                new = jnp.where(here, 0.0, parts[t]) - (columns[t] * r) * row
                if t == own:
                    new = jnp.where(sub > s, new, jnp.where(sub == s, row, parts[t]))
                parts[t] = new
        for t in range(chunks):
            work[group, top + 8 * t : top + 8 * t + 8, :] = parts[t]
        below = top + PANEL
        if below < size:
            rows_id = lax.broadcasted_iota(jnp.int32, (PANEL, size), 0) + top
            lane2 = lax.broadcasted_iota(jnp.int32, (PANEL, size), 1)
            in_panel = (lane2 >= top) & (lane2 < below)
            for g in range(count):
                panel = work[first + g, top:below, :]
                left = panel.T[below:, :]
                right = jnp.where(in_panel & (lane2 > rows_id), 0.0, panel)
                lane3 = lax.broadcasted_iota(jnp.int32, (size - below, size), 1)
                old = work[first + g, below:, :]
                old = jnp.where((lane3 >= top) & (lane3 < below), 0.0, old)
                work[first + g, below:, :] = old - dot(left, right)


def split_factor(w):
    row = lax.broadcasted_iota(jnp.int32, w.shape, 0)
    column = lax.broadcasted_iota(jnp.int32, w.shape, 1)
    upper = jnp.where(row < column, w, jnp.where(row == column, 1.0 / w, 0.0))
    return upper, jnp.where(row >= column, w, 0.0)


def local_kernel(gram_ref, sampled_ref, leaf_ref, local_ref, work):
    leaves = gram_ref.shape[0]
    nodes = 2 * leaves - 1
    rank = gram_ref.shape[-1]
    work[pl.ds(0, leaves)] = gram_ref[...]
    for node in range(leaves, nodes):
        child = 2 * (node - leaves)
        work[node] = work[child] + work[child + 1]
    eliminate(work, 0, leaves)
    eliminate(work, leaves, leaves - 1)
    for leaf in range(leaves):
        leaf_ref[leaf] = dot(sampled_ref[leaf], split_factor(work[leaf])[1], 1, 1)
    for node in range(leaves, nodes):
        child = 2 * (node - leaves)
        inverse = split_factor(work[node])[1]
        for half in range(2):
            factor = split_factor(work[child + half])[0]
            local_ref[node - leaves, half * rank : (half + 1) * rank, :] = dot(
                factor, inverse, 1, 1
            )


def upper_kernel(position, gram_ref, upper_ref, root_ref, work):
    levels = upper_ref.shape[0]
    rank = gram_ref.shape[-1]
    count = 2 * levels + 1
    work[...] = gram_ref[...]
    eliminate(work, 0, count)
    index = position()
    for level in range(levels):
        inverse = split_factor(work[level + 1])[1]
        own = split_factor(work[level])[0]
        partner = split_factor(work[levels + 1 + level])[0]
        second = index // 2**level % 2 == 1
        upper_ref[level, :rank, :] = dot(jnp.where(second, partner, own), inverse, 1, 1)
        upper_ref[level, rank:, :] = dot(jnp.where(second, own, partner), inverse, 1, 1)
    root_ref[...] = split_factor(work[levels])[0]


def per_device(points, tree_order, samples, near_leaves, near_counts):
    leaves = near_counts.shape[0]
    rank_width = samples.shape[1]
    leaf_size = samples.shape[0] // leaves
    sampled, grams = sample_leaves(points, tree_order, samples, near_leaves, near_counts)

    own = grams.reshape(leaves, rank_width, rank_width)
    while own.shape[0] > 1:
        own = own[0::2] + own[1::2]
    own_levels, partner_levels = [own[0]], []
    for axis in ("ty", "tx"):
        for height in range(lax.axis_size(axis).bit_length() - 1):
            partner_levels.append(from_partner(own_levels[-1], axis, height))
            own_levels.append(own_levels[-1] + partner_levels[-1])
    levels = len(partner_levels)

    matrix = (rank_width, rank_width)
    vmem = pl.BlockSpec(memory_space=pltpu.VMEM)
    leaf_basis, local_bases = pl.pallas_call(
        local_kernel,
        out_shape=(
            jax.ShapeDtypeStruct((leaves, leaf_size, rank_width), jnp.float32),
            jax.ShapeDtypeStruct((leaves - 1, 2 * rank_width, rank_width), jnp.float32),
        ),
        in_specs=[vmem, vmem],
        out_specs=(vmem, vmem),
        scratch_shapes=[pltpu.VMEM((2 * leaves - 1, *matrix), jnp.float32)],
        compiler_params=pltpu.CompilerParams(vmem_limit_bytes=32 * 2**20),
        name="local_nodes",
    )(grams, sampled)

    def position():
        return lax.axis_index("tx") * lax.axis_size("ty") + lax.axis_index("ty")

    upper_bases, root = pl.pallas_call(
        functools.partial(upper_kernel, position),
        out_shape=(
            jax.ShapeDtypeStruct((levels, 2 * rank_width, rank_width), jnp.float32),
            jax.ShapeDtypeStruct(matrix, jnp.float32),
        ),
        in_specs=[vmem],
        out_specs=(vmem, vmem),
        scratch_shapes=[pltpu.VMEM((2 * levels + 1, *matrix), jnp.float32)],
        compiler_params=pltpu.CompilerParams(vmem_limit_bytes=32 * 2**20),
        name="upper_nodes",
    )(jnp.stack(own_levels + partner_levels))
    return (leaf_basis.reshape(leaves * leaf_size, rank_width), local_bases, upper_bases, root)


def solution(mesh):
    return jax.shard_map(
        per_device,
        mesh=mesh,
        in_specs=(
            P(None, ("tx", "ty")),
            P(("tx", "ty"), None),
            P(("tx", "ty"), None),
            P(("tx", "ty"), None),
            P(("tx", "ty")),
        ),
        out_specs=(
            P(("tx", "ty"), None),
            P(("tx", "ty"), None, None),
            P(("tx", "ty"), None, None),
            P(),
        ),
        check_vma=False,
    )
```

profile of v0, /device:TPU:0, one launch (start us, length us, event | category | flops | bytes accessed | tf_op | source)
XLA Modules:
  0.0 97.8 jit_solution(97959176432219720)
XLA Ops:
  0.6 0.0 copy-start.1
  0.6 0.0 copy-start.2
  0.7 0.8 copy.11
  1.4 0.0 copy-start.3
  1.4 0.0 copy-done.1
  1.4 0.0 copy-done.2
  1.4 0.6 copy-done.3
  2.1 0.0 copy-start
  2.1 1.2 %copy-done = f32[2048,128]{1,0:T(8,128)S(1)} copy-done((f32[2048,128]{1,0:T(8,128)S(1)}, f32[2048,128]{1,0:T(8,128)}, u32[]{:S(2)}) %copy-start) | copy-done | bytes 1048600
  3.3 28.3 %sample_leaves.1 = (f32[8,256,128]{2,1,0:T(8,128)S(1)}, f32[8,128,128]{2,1,0:T(8,128)S(1)}) custom-call(s32[8,5]{1,0:T(8,128)S(1)} %copy-done.2, s32[8]{0:T(128)S(1)} %copy-done.3, f32[3,16,128]{2,1,0:T(8,128)S(1)} %bitcast.28, s32[16,128]{1,0:T(8,128)S(1)} %bitcast.29, f32[2048,128]{1,0:T(8,128)S(1)} %copy-done), custom_call_target="tpu_custom_call" | custom-call | tf_op jit(solution)/shard_map/sample_leaves/pallas_call | solution.py:217
  31.7 1.6 %collective-permute-start = (f32[128,128]{1,0:T(8,128)S(1)}, f32[128,128]{1,0:T(8,128)S(1)}, u32[]{:S(2)}, u32[]{:S(2)}) collective-permute-start(f32[128,128]{1,0:T(8,128)S(1)} %get-tuple-element.24), channel_id=1, source_target_pairs={{0,1},{1,0},{2,3},{3,2},{4,5},{5,4},{6,7},{7,6},{8,9},{9,8},{10,11... | collective-permute-start | bytes 196616 | tf_op jit(solution)/shard_map/ppermute | solution.py:21
  33.3 2.7 %collective-permute-done = f32[128,128]{1,0:T(8,128)S(1)} collective-permute-done((f32[128,128]{1,0:T(8,128)S(1)}, f32[128,128]{1,0:T(8,128)S(1)}, u32[]{:S(2)}, u32[]{:S(2)}) %collective-permute-start) | collective-permute-done | bytes 65568 | tf_op jit(solution)/shard_map/ppermute | solution.py:21
  36.0 2.6 %collective-permute-start.1 = (f32[128,128]{1,0:T(8,128)S(1)}, f32[128,128]{1,0:T(8,128)S(1)}, u32[]{:S(2)}, u32[]{:S(2)}) collective-permute-start(f32[128,128]{1,0:T(8,128)S(1)} %get-tuple-element.23), channel_id=1, source_target_pairs={{0,2},{1,3},{2,0},{3,1},{4,6},{5,7},{6,4},{7,5},{8,10},{9,11},{10,... | collective-permute-start | bytes 196616 | tf_op jit(solution)/shard_map/ppermute | solution.py:21
  38.6 4.4 %collective-permute-done.1 = f32[128,128]{1,0:T(8,128)S(1)} collective-permute-done((f32[128,128]{1,0:T(8,128)S(1)}, f32[128,128]{1,0:T(8,128)S(1)}, u32[]{:S(2)}, u32[]{:S(2)}) %collective-permute-start.1) | collective-permute-done | bytes 65568 | tf_op jit(solution)/shard_map/ppermute | solution.py:21
  43.0 0.1 collective-permute-start.2
  43.1 1.2 %collective-permute-done.2 = f32[128,128]{1,0:T(8,128)S(1)} collective-permute-done((f32[128,128]{1,0:T(8,128)S(1)}, f32[128,128]{1,0:T(8,128)S(1)}, u32[]{:S(2)}, u32[]{:S(2)}) %collective-permute-start.2) | collective-permute-done | bytes 65568 | tf_op jit(solution)/shard_map/ppermute | solution.py:21
  44.3 2.4 %collective-permute-start.3 = (f32[128,128]{1,0:T(8,128)S(1)}, f32[128,128]{1,0:T(8,128)S(1)}, u32[]{:S(2)}, u32[]{:S(2)}) collective-permute-start(f32[128,128]{1,0:T(8,128)S(1)} %get-tuple-element.19), channel_id=1, source_target_pairs={{0,8},{4,12},{8,0},{12,4},{16,24},{20,28},{24,16},{28,20},{1,9},{5... | collective-permute-start | bytes 196616 | tf_op jit(solution)/shard_map/ppermute | solution.py:21
  46.8 2.4 %collective-permute-done.3 = f32[128,128]{1,0:T(8,128)S(1)} collective-permute-done((f32[128,128]{1,0:T(8,128)S(1)}, f32[128,128]{1,0:T(8,128)S(1)}, u32[]{:S(2)}, u32[]{:S(2)}) %collective-permute-start.3) | collective-permute-done | bytes 65568 | tf_op jit(solution)/shard_map/ppermute | solution.py:21
  49.2 1.1 %collective-permute-start.4 = (f32[128,128]{1,0:T(8,128)S(1)}, f32[128,128]{1,0:T(8,128)S(1)}, u32[]{:S(2)}, u32[]{:S(2)}) collective-permute-start(f32[128,128]{1,0:T(8,128)S(1)} %get-tuple-element.17), channel_id=1, source_target_pairs={{0,16},{4,20},{8,24},{12,28},{16,0},{20,4},{24,8},{28,12},{1,17},{... | collective-permute-start | bytes 196616 | tf_op jit(solution)/shard_map/ppermute | solution.py:21
  50.2 28.8 %local_nodes.1 = (f32[8,256,128]{2,1,0:T(8,128)}, f32[7,256,128]{2,1,0:T(8,128)}) custom-call(f32[8,128,128]{2,1,0:T(8,128)S(1)} %get-tuple-element.10.gram_ref, f32[8,256,128]{2,1,0:T(8,128)S(1)} %get-tuple-element.11.sampled_ref), custom_call_target="tpu_custom_call" | custom-call | tf_op jit(solution)/shard_map/local_nodes/pallas_call | solution.py:356
  79.1 0.0 collective-permute-done.4
  79.2 18.6 %upper_nodes.1 = (f32[5,256,128]{2,1,0:T(8,128)}, f32[128,128]{1,0:T(8,128)}) custom-call(f32[11,128,128]{2,1,0:T(8,128)S(1)} %bitcast_dynamic-update-slice_fusion.gram_ref), custom_call_target="tpu_custom_call" | custom-call | tf_op jit(solution)/shard_map/upper_nodes/pallas_call | solution.py:372
  (13 shorter events, 0.1 us)
Async XLA Ops:
  0.6 0.8 copy-start.1
  0.6 0.8 copy-start.2
  1.4 0.7 copy-start.3
  2.1 1.2 %copy-start = (f32[2048,128]{1,0:T(8,128)S(1)}, f32[2048,128]{1,0:T(8,128)}, u32[]{:S(2)}) copy-start(f32[2048,128]{1,0:T(8,128)} %samples_ref.1) | copy-start | bytes 3145732
  31.7 4.3 %collective-permute-start = (f32[128,128]{1,0:T(8,128)S(1)}, f32[128,128]{1,0:T(8,128)S(1)}, u32[]{:S(2)}, u32[]{:S(2)}) collective-permute-start(f32[128,128]{1,0:T(8,128)S(1)} %get-tuple-element.24), channel_id=1, source_target_pairs={{0,1},{1,0},{2,3},{3,2},{4,5},{5,4},{6,7},{7,6},{8,9},{9,8},{10,11... | collective-permute-start | bytes 196616 | tf_op jit(solution)/shard_map/ppermute | solution.py:21
  36.0 6.9 %collective-permute-start.1 = (f32[128,128]{1,0:T(8,128)S(1)}, f32[128,128]{1,0:T(8,128)S(1)}, u32[]{:S(2)}, u32[]{:S(2)}) collective-permute-start(f32[128,128]{1,0:T(8,128)S(1)} %get-tuple-element.23), channel_id=1, source_target_pairs={{0,2},{1,3},{2,0},{3,1},{4,6},{5,7},{6,4},{7,5},{8,10},{9,11},{10,... | collective-permute-start | bytes 196616 | tf_op jit(solution)/shard_map/ppermute | solution.py:21
  43.0 1.3 %collective-permute-start.2 = (f32[128,128]{1,0:T(8,128)S(1)}, f32[128,128]{1,0:T(8,128)S(1)}, u32[]{:S(2)}, u32[]{:S(2)}) collective-permute-start(f32[128,128]{1,0:T(8,128)S(1)} %get-tuple-element.21), channel_id=1, source_target_pairs={{0,4},{4,0},{8,12},{12,8},{16,20},{20,16},{24,28},{28,24},{1,5},{5... | collective-permute-start | bytes 196616 | tf_op jit(solution)/shard_map/ppermute | solution.py:21
  44.3 4.9 %collective-permute-start.3 = (f32[128,128]{1,0:T(8,128)S(1)}, f32[128,128]{1,0:T(8,128)S(1)}, u32[]{:S(2)}, u32[]{:S(2)}) collective-permute-start(f32[128,128]{1,0:T(8,128)S(1)} %get-tuple-element.19), channel_id=1, source_target_pairs={{0,8},{4,12},{8,0},{12,4},{16,24},{20,28},{24,16},{28,20},{1,9},{5... | collective-permute-start | bytes 196616 | tf_op jit(solution)/shard_map/ppermute | solution.py:21
  49.2 29.9 %collective-permute-start.4 = (f32[128,128]{1,0:T(8,128)S(1)}, f32[128,128]{1,0:T(8,128)S(1)}, u32[]{:S(2)}, u32[]{:S(2)}) collective-permute-start(f32[128,128]{1,0:T(8,128)S(1)} %get-tuple-element.17), channel_id=1, source_target_pairs={{0,16},{4,20},{8,24},{12,28},{16,0},{20,4},{24,8},{28,12},{1,17},{... | collective-permute-start | bytes 196616 | tf_op jit(solution)/shard_map/ppermute | solution.py:21
where the time goes:
time: 98.1 us; the launch traced here: 97.8 us
  Pallas kernels  75.8 us (77%)
  waiting for transfers between devices  10.7 us (11%)
  starting transfers between devices  7.77 us (8%)
  local copies, waits for them, and re-layouts  2.69 us (3%)
    pallas_call x1, Pallas kernels, per_device(): pl.pallas_call(local_kernel, out_shape=(jax.ShapeDtypeStruct((leaves, lea...  28.8 us
    pallas_call x1, Pallas kernels, sample_leaves(): pl.pallas_call(sample_kernel, out_shape=(jax.ShapeDtypeStruct((leaves, le...  28.3 us
    pallas_call x1, Pallas kernels, per_device(): pl.pallas_call(functools.partial(upper_kernel, position), out_shape=(jax....  18.6 us
    ppermute x5, waiting for transfers between devices, from_partner(): return lax.ppermute(value, axis, pairs)  10.7 us
    ppermute x5, starting transfers between devices, from_partner(): return lax.ppermute(value, axis, pairs)  7.77 us
    unnamed x13, local copies, waits for them, and re-layouts  2.68 us
  transfers between devices with their start and end apart: 5, of which 4 were waited for; matrix products, arithmetic and copies ran while one was open for 0% of the time, Pallas kernels for 29%

commit v1 on v0

--- a/solution.py
+++ b/solution.py
@@ -13,12 +13,6 @@
 
 
 SPREAD = 50.0
-
-
-def from_partner(value, axis, stride):
-    mask = 2**stride
-    pairs = [(source, source ^ mask) for source in range(lax.axis_size(axis))]
-    return lax.ppermute(value, axis, pairs)
 
 
 def dot(a, b, contract_a=1, contract_b=0):
@@ -248,45 +242,70 @@
     )
 
 
+def three_terms(x):
+    high = x.astype(jnp.bfloat16)
+    rest = x - high.astype(jnp.float32)
+    middle = rest.astype(jnp.bfloat16)
+    low = (rest - middle.astype(jnp.float32)).astype(jnp.bfloat16)
+    return high, middle, low
+
+
+def gram_product(left, right):
+    a, b, c = three_terms(left)
+    d, e, f = three_terms(right)
+    return lax.dot_general(
+        jnp.concatenate([a, a, b, a, b, c], axis=0),
+        jnp.concatenate([d, e, d, f, e, d], axis=0),
+        (((0,), (0,)), ((), ())),
+        preferred_element_type=jnp.float32,
+    )
+
+
 def eliminate(work, first, count):
     size = work.shape[-1]
     chunks = PANEL // 8
-    lane = lax.broadcasted_iota(jnp.int32, (1, 1, size), 2)
+    lane = lax.broadcasted_iota(jnp.int32, (1, 8, size), 2)
     sub = lax.broadcasted_iota(jnp.int32, (1, 8, size), 1)
     group = pl.ds(first, count)
     for top in range(0, size, PANEL):
         parts = [work[group, top + 8 * t : top + 8 * t + 8, :] for t in range(chunks)]
-        for k in range(PANEL):
-            own, s = k // 8, k % 8
-            here = lane == top + k
-            columns = {
-                t: jnp.broadcast_to(parts[t][:, :, top + k : top + k + 1], parts[t].shape)
-                for t in range(own, chunks)
-            }
-            d = columns[own][:, s : s + 1, :]
-            r = lax.rsqrt(d)
-            r = r * (1.5 - 0.5 * d * r * r)
-            row = jnp.where(here, r, parts[own][:, s : s + 1, :] * r)
-            for t in range(own, chunks):
-                new = jnp.where(here, 0.0, parts[t]) - (columns[t] * r) * row
-                if t == own:
-                    new = jnp.where(sub > s, new, jnp.where(sub == s, row, parts[t]))
-                parts[t] = new
-        for t in range(chunks):
-            work[group, top + 8 * t : top + 8 * t + 8, :] = parts[t]
+        for own in range(chunks):
+            pivots = jnp.ones_like(parts[own])
+            for s in range(8):
+                k = top + 8 * own + s
+                here = lane == k
+                columns = [
+                    jnp.broadcast_to(parts[t][:, :, k : k + 1], parts[t].shape)
+                    for t in range(own, chunks)
+                ]
+                d = columns[0][:, s : s + 1, :]
+                inverse = pl.reciprocal(d, approx=True)
+                inverse = inverse * (2.0 - d * inverse)
+                pivots = jnp.where(sub == s, d, pivots)
+                row = jnp.where(here[:, :1], 1.0, parts[own][:, s : s + 1, :])
+                for t in range(own, chunks):
+                    step = (columns[t - own] * row) * inverse
+                    if t == own:
+                        step = jnp.where(sub > s, step, 0.0)
+                        kept = jnp.where(sub == s, 1.0, 0.0)
+                        parts[t] = jnp.where(here & (sub >= s), kept, parts[t]) - step
+                    else:
+                        parts[t] = jnp.where(here, 0.0, parts[t]) - step
+            scale = lax.rsqrt(pivots)
+            scale = scale * (1.5 - 0.5 * pivots * scale * scale)
+            work[group, top + 8 * own : top + 8 * own + 8, :] = parts[own] * scale
         below = top + PANEL
         if below < size:
             rows_id = lax.broadcasted_iota(jnp.int32, (PANEL, size), 0) + top
             lane2 = lax.broadcasted_iota(jnp.int32, (PANEL, size), 1)
             in_panel = (lane2 >= top) & (lane2 < below)
+            lane3 = lax.broadcasted_iota(jnp.int32, (size - below, size), 1)
+            cleared = (lane3 >= top) & (lane3 < below)
             for g in range(count):
                 panel = work[first + g, top:below, :]
-                left = panel.T[below:, :]
                 right = jnp.where(in_panel & (lane2 > rows_id), 0.0, panel)
-                lane3 = lax.broadcasted_iota(jnp.int32, (size - below, size), 1)
-                old = work[first + g, below:, :]
-                old = jnp.where((lane3 >= top) & (lane3 < below), 0.0, old)
-                work[first + g, below:, :] = old - dot(left, right)
+                old = jnp.where(cleared, 0.0, work[first + g, below:, :])
+                work[first + g, below:, :] = old - gram_product(panel, right)[below:]
 
 
 def split_factor(w):
@@ -296,18 +315,82 @@
     return upper, jnp.where(row >= column, w, 0.0)
 
 
-def local_kernel(gram_ref, sampled_ref, leaf_ref, local_ref, work):
+def node_kernel(
+    gram_ref, sampled_ref, leaf_ref, local_ref, upper_ref, root_ref,
+    work, sums, partner_sums, factors, partner_factors,
+    sum_send, sum_recv, factor_send, factor_recv,
+):
     leaves = gram_ref.shape[0]
     nodes = 2 * leaves - 1
     rank = gram_ref.shape[-1]
+    levels = upper_ref.shape[0]
+    me = linear_position()
+
+    def partner(level):
+        return device_at(me + (1 - me // 2**level % 2 * 2) * 2**level)
+
+    barrier = pltpu.get_barrier_semaphore()
+    for level in range(levels):
+        pl.semaphore_signal(
+            barrier, inc=1, device_id=partner(level), device_id_type=pl.DeviceIdType.MESH
+        )
+
     work[pl.ds(0, leaves)] = gram_ref[...]
     for node in range(leaves, nodes):
         child = 2 * (node - leaves)
         work[node] = work[child] + work[child + 1]
-    eliminate(work, 0, leaves)
-    eliminate(work, leaves, leaves - 1)
-    for leaf in range(leaves):
+    sums[0] = work[nodes - 1]
+    pl.semaphore_wait(barrier, levels)
+
+    def copy(level, source, target, send, recv):
+        return pltpu.make_async_remote_copy(
+            src_ref=source.at[level],
+            dst_ref=target.at[level],
+            send_sem=send.at[level],
+            recv_sem=recv.at[level],
+            device_id=partner(level),
+            device_id_type=pl.DeviceIdType.MESH,
+        )
+
+    sum_copies = [copy(h, sums, partner_sums, sum_send, sum_recv) for h in range(levels)]
+    factor_copies = [
+        copy(h, factors, partner_factors, factor_send, factor_recv) for h in range(levels)
+    ]
+
+    def climb(level):
+        if level < levels:
+            sum_copies[level].wait_recv()
+            sums[level + 1] = sums[level] + partner_sums[level]
+            if level + 1 < levels:
+                sum_copies[level + 1].start()
+
+    def leaf_basis(leaf):
         leaf_ref[leaf] = dot(sampled_ref[leaf], split_factor(work[leaf])[1], 1, 1)
+
+    sum_copies[0].start()
+    group = max(g for g in range(1, 6) if nodes % g == 0)
+    groups = nodes // group
+
+    @pl.loop(0, groups)
+    def _(g):
+        eliminate(work, g * group, group)
+        for level in range(min(groups, levels)):
+            pl.when(g == level)(functools.partial(climb, level))
+
+    for leaf in range(leaves // 2):
+        leaf_basis(leaf)
+    climb(groups)
+    for leaf in range(leaves // 2, leaves):
+        leaf_basis(leaf)
+    for level in range(groups + 1, levels):
+        climb(level)
+    factors[0] = work[nodes - 1]
+    for level in range(1, levels + 1):
+        factors[level] = sums[level]
+    eliminate(factors, 1, levels)
+    for c in factor_copies:
+        c.start()
+    root_ref[...] = split_factor(factors[levels])[0]
     for node in range(leaves, nodes):
         child = 2 * (node - leaves)
         inverse = split_factor(work[node])[1]
@@ -316,23 +399,16 @@
             local_ref[node - leaves, half * rank : (half + 1) * rank, :] = dot(
                 factor, inverse, 1, 1
             )
-
-
-def upper_kernel(position, gram_ref, upper_ref, root_ref, work):
-    levels = upper_ref.shape[0]
-    rank = gram_ref.shape[-1]
-    count = 2 * levels + 1
-    work[...] = gram_ref[...]
-    eliminate(work, 0, count)
-    index = position()
     for level in range(levels):
-        inverse = split_factor(work[level + 1])[1]
-        own = split_factor(work[level])[0]
-        partner = split_factor(work[levels + 1 + level])[0]
-        second = index // 2**level % 2 == 1
-        upper_ref[level, :rank, :] = dot(jnp.where(second, partner, own), inverse, 1, 1)
-        upper_ref[level, rank:, :] = dot(jnp.where(second, own, partner), inverse, 1, 1)
-    root_ref[...] = split_factor(work[levels])[0]
+        factor_copies[level].wait_recv()
+        inverse = split_factor(factors[level + 1])[1]
+        own = split_factor(factors[level])[0]
+        other = split_factor(partner_factors[level])[0]
+        second = me // 2**level % 2 == 1
+        upper_ref[level, :rank, :] = dot(jnp.where(second, other, own), inverse, 1, 1)
+        upper_ref[level, rank:, :] = dot(jnp.where(second, own, other), inverse, 1, 1)
+    for c in sum_copies + factor_copies:
+        c.wait_send()
 
 
 def per_device(points, tree_order, samples, near_leaves, near_counts):
@@ -341,46 +417,33 @@
     leaf_size = samples.shape[0] // leaves
     sampled, grams = sample_leaves(points, tree_order, samples, near_leaves, near_counts)
 
-    own = grams.reshape(leaves, rank_width, rank_width)
-    while own.shape[0] > 1:
-        own = own[0::2] + own[1::2]
-    own_levels, partner_levels = [own[0]], []
-    for axis in ("ty", "tx"):
-        for height in range(lax.axis_size(axis).bit_length() - 1):
-            partner_levels.append(from_partner(own_levels[-1], axis, height))
-            own_levels.append(own_levels[-1] + partner_levels[-1])
-    levels = len(partner_levels)
-
+    devices = lax.axis_size("tx") * lax.axis_size("ty")
+    levels = devices.bit_length() - 1
     matrix = (rank_width, rank_width)
     vmem = pl.BlockSpec(memory_space=pltpu.VMEM)
-    leaf_basis, local_bases = pl.pallas_call(
-        local_kernel,
+    leaf_basis, local_bases, upper_bases, root = pl.pallas_call(
+        node_kernel,
         out_shape=(
             jax.ShapeDtypeStruct((leaves, leaf_size, rank_width), jnp.float32),
             jax.ShapeDtypeStruct((leaves - 1, 2 * rank_width, rank_width), jnp.float32),
-        ),
-        in_specs=[vmem, vmem],
-        out_specs=(vmem, vmem),
-        scratch_shapes=[pltpu.VMEM((2 * leaves - 1, *matrix), jnp.float32)],
-        compiler_params=pltpu.CompilerParams(vmem_limit_bytes=32 * 2**20),
-        name="local_nodes",
-    )(grams, sampled)
-
-    def position():
-        return lax.axis_index("tx") * lax.axis_size("ty") + lax.axis_index("ty")
-
-    upper_bases, root = pl.pallas_call(
-        functools.partial(upper_kernel, position),
-        out_shape=(
             jax.ShapeDtypeStruct((levels, 2 * rank_width, rank_width), jnp.float32),
             jax.ShapeDtypeStruct(matrix, jnp.float32),
         ),
-        in_specs=[vmem],
-        out_specs=(vmem, vmem),
-        scratch_shapes=[pltpu.VMEM((2 * levels + 1, *matrix), jnp.float32)],
-        compiler_params=pltpu.CompilerParams(vmem_limit_bytes=32 * 2**20),
-        name="upper_nodes",
-    )(jnp.stack(own_levels + partner_levels))
+        in_specs=[vmem, vmem],
+        out_specs=(vmem,) * 4,
+        scratch_shapes=[
+            pltpu.VMEM((2 * leaves - 1, *matrix), jnp.float32),
+            pltpu.VMEM((levels + 1, *matrix), jnp.float32),
+            pltpu.VMEM((levels, *matrix), jnp.float32),
+            pltpu.VMEM((levels + 1, *matrix), jnp.float32),
+            pltpu.VMEM((levels, *matrix), jnp.float32),
+        ]
+        + [pltpu.SemaphoreType.DMA((levels,))] * 4,
+        compiler_params=pltpu.CompilerParams(
+            vmem_limit_bytes=40 * 2**20, collective_id=1, has_side_effects=True
+        ),
+        name="tree_nodes",
+    )(grams, sampled)
     return (leaf_basis.reshape(leaves * leaf_size, rank_width), local_bases, upper_bases, root)
 
 

time: 98.1 us -> 102 us (1.040)
  Pallas kernels: 75.8 us -> 94.9 us
  waiting for transfers between devices: 10.7 us -> 0 us
  starting transfers between devices: 7.77 us -> 0 us
  local copies, waits for them, and re-layouts: 2.69 us -> 6.01 us
    pallas_call x2 -> x1, Pallas kernels: 47.5 us -> 66.8 us  [per_device(): pl.pallas_call(node_kernel, out_shape=(jax.ShapeDtypeStruct((leaves, leaf...]
    ppermute x5 -> x0, waiting for transfers between devices: 10.7 us -> none  [from_partner(): return lax.ppermute(value, axis, pairs)]
    ppermute x5 -> x0, starting transfers between devices: 7.77 us -> none  [from_partner(): return lax.ppermute(value, axis, pairs)]
    unnamed x13, local copies, waits for them, and re-layouts: 2.68 us -> 6.01 us
  transfers between devices with their start and end apart: 5 -> 0, of which waited for: 4 -> 0; matrix products, arithmetic and copies ran while one was open for 0% -> 0% of each run, Pallas kernels for 29% -> 0%
where the time goes in v1:
time: 102 us
  Pallas kernels  94.9 us (93%)
  local copies, waits for them, and re-layouts  6.01 us (6%)
    pallas_call x1, Pallas kernels, per_device(): pl.pallas_call(node_kernel, out_shape=(jax.ShapeDtypeStruct((leaves, leaf...  66.8 us
    pallas_call x1, Pallas kernels, sample_leaves(): pl.pallas_call(sample_kernel, out_shape=(jax.ShapeDtypeStruct((leaves, le...  28.1 us
    unnamed x13, local copies, waits for them, and re-layouts  6.01 us

profile of v1, /device:TPU:0, one launch (start us, length us, event | category | flops | bytes accessed | tf_op | source)
XLA Modules:
  0.0 101.6 jit_solution(9347187201318392981)
XLA Ops:
  0.6 0.0 copy-start.1
  0.6 0.0 copy-start.2
  0.7 0.8 copy.11
  1.4 0.0 copy-start.3
  1.4 0.0 copy-done.1
  1.4 0.0 copy-done.2
  1.4 0.6 copy-done.3
  2.1 0.0 copy-start
  2.1 1.2 %copy-done = f32[2048,128]{1,0:T(8,128)S(1)} copy-done((f32[2048,128]{1,0:T(8,128)S(1)}, f32[2048,128]{1,0:T(8,128)}, u32[]{:S(2)}) %copy-start) | copy-done | bytes 1048600
  3.3 28.1 %sample_leaves.1 = (f32[8,256,128]{2,1,0:T(8,128)S(1)}, f32[8,128,128]{2,1,0:T(8,128)S(1)}) custom-call(s32[8,5]{1,0:T(8,128)S(1)} %copy-done.2, s32[8]{0:T(128)S(1)} %copy-done.3, f32[3,16,128]{2,1,0:T(8,128)S(1)} %bitcast.7, s32[16,128]{1,0:T(8,128)S(1)} %bitcast.8, f32[2048,128]{1,0:T(8,128)S(1)} %copy-done), custom_call_target="tpu_custom_call" | custom-call | tf_op jit(solution)/shard_map/sample_leaves/pallas_call | solution.py:211
  31.4 66.8 %tree_nodes.1 = (f32[8,256,128]{2,1,0:T(8,128)S(1)}, f32[7,256,128]{2,1,0:T(8,128)S(1)}, f32[5,256,128]{2,1,0:T(8,128)S(1)}, f32[128,128]{1,0:T(8,128)S(1)}) custom-call(f32[8,128,128]{2,1,0:T(8,128)S(1)} %get-tuple-element.10.gram_ref, f32[8,256,128]{2,1,0:T(8,128)S(1)} %get-tuple-element.11.sampled_ref), custom_call_target="tpu_custom_call" | custom-call | tf_op jit(solution)/shard_map/tree_nodes/pallas_call | solution.py:424
  98.2 1.0 copy.16
  99.2 0.9 copy.17
  100.1 0.8 copy.18
  100.9 0.6 copy.19
Async XLA Ops:
  0.6 0.8 copy-start.1
  0.6 0.8 copy-start.2
  1.4 0.7 copy-start.3
  2.1 1.2 %copy-start = (f32[2048,128]{1,0:T(8,128)S(1)}, f32[2048,128]{1,0:T(8,128)}, u32[]{:S(2)}) copy-start(f32[2048,128]{1,0:T(8,128)} %samples_ref.1) | copy-start | bytes 3145732

commit v2 on v1

--- a/solution.py
+++ b/solution.py
@@ -242,70 +242,45 @@
     )
 
 
-def three_terms(x):
-    high = x.astype(jnp.bfloat16)
-    rest = x - high.astype(jnp.float32)
-    middle = rest.astype(jnp.bfloat16)
-    low = (rest - middle.astype(jnp.float32)).astype(jnp.bfloat16)
-    return high, middle, low
-
-
-def gram_product(left, right):
-    a, b, c = three_terms(left)
-    d, e, f = three_terms(right)
-    return lax.dot_general(
-        jnp.concatenate([a, a, b, a, b, c], axis=0),
-        jnp.concatenate([d, e, d, f, e, d], axis=0),
-        (((0,), (0,)), ((), ())),
-        preferred_element_type=jnp.float32,
-    )
-
-
 def eliminate(work, first, count):
     size = work.shape[-1]
     chunks = PANEL // 8
-    lane = lax.broadcasted_iota(jnp.int32, (1, 8, size), 2)
+    lane = lax.broadcasted_iota(jnp.int32, (1, 1, size), 2)
     sub = lax.broadcasted_iota(jnp.int32, (1, 8, size), 1)
     group = pl.ds(first, count)
     for top in range(0, size, PANEL):
         parts = [work[group, top + 8 * t : top + 8 * t + 8, :] for t in range(chunks)]
-        for own in range(chunks):
-            pivots = jnp.ones_like(parts[own])
-            for s in range(8):
-                k = top + 8 * own + s
-                here = lane == k
-                columns = [
-                    jnp.broadcast_to(parts[t][:, :, k : k + 1], parts[t].shape)
-                    for t in range(own, chunks)
-                ]
-                d = columns[0][:, s : s + 1, :]
-                inverse = pl.reciprocal(d, approx=True)
-                inverse = inverse * (2.0 - d * inverse)
-                pivots = jnp.where(sub == s, d, pivots)
-                row = jnp.where(here[:, :1], 1.0, parts[own][:, s : s + 1, :])
-                for t in range(own, chunks):
-                    step = (columns[t - own] * row) * inverse
-                    if t == own:
-                        step = jnp.where(sub > s, step, 0.0)
-                        kept = jnp.where(sub == s, 1.0, 0.0)
-                        parts[t] = jnp.where(here & (sub >= s), kept, parts[t]) - step
-                    else:
-                        parts[t] = jnp.where(here, 0.0, parts[t]) - step
-            scale = lax.rsqrt(pivots)
-            scale = scale * (1.5 - 0.5 * pivots * scale * scale)
-            work[group, top + 8 * own : top + 8 * own + 8, :] = parts[own] * scale
+        for k in range(PANEL):
+            own, s = k // 8, k % 8
+            here = lane == top + k
+            columns = {
+                t: jnp.broadcast_to(parts[t][:, :, top + k : top + k + 1], parts[t].shape)
+                for t in range(own, chunks)
+            }
+            d = columns[own][:, s : s + 1, :]
+            r = lax.rsqrt(d)
+            r = r * (1.5 - 0.5 * d * r * r)
+            row = jnp.where(here, r, parts[own][:, s : s + 1, :] * r)
+            for t in range(own, chunks):
+                new = jnp.where(here, 0.0, parts[t]) - (columns[t] * r) * row
+                if t == own:
+                    new = jnp.where(sub > s, new, jnp.where(sub == s, row, parts[t]))
+                parts[t] = new
+        for t in range(chunks):
+            work[group, top + 8 * t : top + 8 * t + 8, :] = parts[t]
         below = top + PANEL
         if below < size:
             rows_id = lax.broadcasted_iota(jnp.int32, (PANEL, size), 0) + top
             lane2 = lax.broadcasted_iota(jnp.int32, (PANEL, size), 1)
             in_panel = (lane2 >= top) & (lane2 < below)
-            lane3 = lax.broadcasted_iota(jnp.int32, (size - below, size), 1)
-            cleared = (lane3 >= top) & (lane3 < below)
             for g in range(count):
                 panel = work[first + g, top:below, :]
+                left = panel.T[below:, :]
                 right = jnp.where(in_panel & (lane2 > rows_id), 0.0, panel)
-                old = jnp.where(cleared, 0.0, work[first + g, below:, :])
-                work[first + g, below:, :] = old - gram_product(panel, right)[below:]
+                lane3 = lax.broadcasted_iota(jnp.int32, (size - below, size), 1)
+                old = work[first + g, below:, :]
+                old = jnp.where((lane3 >= top) & (lane3 < below), 0.0, old)
+                work[first + g, below:, :] = old - dot(left, right)
 
 
 def split_factor(w):
@@ -367,22 +342,30 @@
     def leaf_basis(leaf):
         leaf_ref[leaf] = dot(sampled_ref[leaf], split_factor(work[leaf])[1], 1, 1)
 
+    def node_basis(node):
+        child = 2 * (node - leaves)
+        inverse = split_factor(work[node])[1]
+        for half in range(2):
+            factor = split_factor(work[child + half])[0]
+            local_ref[node - leaves, half * rank : (half + 1) * rank, :] = dot(
+                factor, inverse, 1, 1
+            )
+
     sum_copies[0].start()
-    group = max(g for g in range(1, 6) if nodes % g == 0)
-    groups = nodes // group
-
-    @pl.loop(0, groups)
-    def _(g):
-        eliminate(work, g * group, group)
-        for level in range(min(groups, levels)):
-            pl.when(g == level)(functools.partial(climb, level))
-
+    eliminate(work, 0, leaves)
+    climb(0)
     for leaf in range(leaves // 2):
         leaf_basis(leaf)
-    climb(groups)
+    climb(1)
     for leaf in range(leaves // 2, leaves):
         leaf_basis(leaf)
-    for level in range(groups + 1, levels):
+    climb(2)
+    eliminate(work, leaves, leaves - 1)
+    climb(3)
+    middle = leaves + leaves // 2
+    for node in range(leaves, middle):
+        node_basis(node)
+    for level in range(4, levels):
         climb(level)
     factors[0] = work[nodes - 1]
     for level in range(1, levels + 1):
@@ -391,14 +374,8 @@
     for c in factor_copies:
         c.start()
     root_ref[...] = split_factor(factors[levels])[0]
-    for node in range(leaves, nodes):
-        child = 2 * (node - leaves)
-        inverse = split_factor(work[node])[1]
-        for half in range(2):
-            factor = split_factor(work[child + half])[0]
-            local_ref[node - leaves, half * rank : (half + 1) * rank, :] = dot(
-                factor, inverse, 1, 1
-            )
+    for node in range(middle, nodes):
+        node_basis(node)
     for level in range(levels):
         factor_copies[level].wait_recv()
         inverse = split_factor(factors[level + 1])[1]

time: 102 us -> 101 us (level)
    pallas_call x1, Pallas kernels: 66.8 us -> 65.8 us  [per_device(): pl.pallas_call(node_kernel, out_shape=(jax.ShapeDtypeStruct((leaves, leaf...]
where the time goes in v2:
time: 101 us
  Pallas kernels  94 us (93%)
  local copies, waits for them, and re-layouts  6.01 us (6%)
    pallas_call x1, Pallas kernels, per_device(): pl.pallas_call(node_kernel, out_shape=(jax.ShapeDtypeStruct((leaves, leaf...  65.8 us
    pallas_call x1, Pallas kernels, sample_leaves(): pl.pallas_call(sample_kernel, out_shape=(jax.ShapeDtypeStruct((leaves, le...  28.2 us
    unnamed x13, local copies, waits for them, and re-layouts  6.01 us

profile of v2, /device:TPU:0, one launch (start us, length us, event | category | flops | bytes accessed | tf_op | source)
XLA Modules:
  0.0 100.7 jit_solution(4029692674542916499)
XLA Ops:
  0.6 0.0 copy-start.1
  0.6 0.0 copy-start.2
  0.7 0.8 copy.11
  1.4 0.0 copy-start.3
  1.4 0.0 copy-done.1
  1.4 0.0 copy-done.2
  1.4 0.6 copy-done.3
  2.1 0.0 copy-start
  2.1 1.2 %copy-done = f32[2048,128]{1,0:T(8,128)S(1)} copy-done((f32[2048,128]{1,0:T(8,128)S(1)}, f32[2048,128]{1,0:T(8,128)}, u32[]{:S(2)}) %copy-start) | copy-done | bytes 1048600
  3.3 28.2 %sample_leaves.1 = (f32[8,256,128]{2,1,0:T(8,128)S(1)}, f32[8,128,128]{2,1,0:T(8,128)S(1)}) custom-call(s32[8,5]{1,0:T(8,128)S(1)} %copy-done.2, s32[8]{0:T(128)S(1)} %copy-done.3, f32[3,16,128]{2,1,0:T(8,128)S(1)} %bitcast.7, s32[16,128]{1,0:T(8,128)S(1)} %bitcast.8, f32[2048,128]{1,0:T(8,128)S(1)} %copy-done), custom_call_target="tpu_custom_call" | custom-call | tf_op jit(solution)/shard_map/sample_leaves/pallas_call | solution.py:211
  31.5 65.8 %tree_nodes.1 = (f32[8,256,128]{2,1,0:T(8,128)S(1)}, f32[7,256,128]{2,1,0:T(8,128)S(1)}, f32[5,256,128]{2,1,0:T(8,128)S(1)}, f32[128,128]{1,0:T(8,128)S(1)}) custom-call(f32[8,128,128]{2,1,0:T(8,128)S(1)} %get-tuple-element.10.gram_ref, f32[8,256,128]{2,1,0:T(8,128)S(1)} %get-tuple-element.11.sampled_ref), custom_call_target="tpu_custom_call" | custom-call | tf_op jit(solution)/shard_map/tree_nodes/pallas_call | solution.py:401
  97.3 1.0 copy.16
  98.3 0.9 copy.17
  99.2 0.8 copy.18
  100.0 0.6 copy.19
Async XLA Ops:
  0.6 0.8 copy-start.1
  0.6 0.8 copy-start.2
  1.4 0.7 copy-start.3
  2.1 1.2 %copy-start = (f32[2048,128]{1,0:T(8,128)S(1)}, f32[2048,128]{1,0:T(8,128)}, u32[]{:S(2)}) copy-start(f32[2048,128]{1,0:T(8,128)} %samples_ref.1) | copy-start | bytes 3145732
